TPU v7x, 256 devices: a whole 4x4x8 slice. The times are simulated.
256 devices in a mesh: adapter: 32 (over y, x, core), tensor: 8 (over z).
Axes of the slice: x: 4, y: 4, z: 8, core: 2. Of those that a mesh axis runs over, the one named last changes fastest.
Arguments:
- attended: bfloat16 [4096, 8192], P('adapter'), may hold values from -6 to 6
- residual: bfloat16 [4096, 8192], P('adapter', 'tensor'), may hold values from -6 to 6
- output_matrix: bfloat16 [8192, 8192], P('adapter', 'tensor'), may hold values from -0.0625 to 0.0625
- adapter_down_weight: bfloat16 [512, 64, 8192], P('adapter', None, 'tensor'), may hold values from -0.0625 to 0.0625
- adapter_up_weight: bfloat16 [512, 64, 8192], P('adapter', None, 'tensor'), may hold values from -0.75 to 0.75
- request_adapter_index: int32 [4096], P('adapter'), may hold values from 0 to 511, as said below
Outputs:
- layer_out: bfloat16 [4096, 8192], P('adapter', 'tensor')
Inputs may be any that keep to these rules, and one draw needn't show every extreme that they name: `request_adapter_index`: the owner of adapter id is id // 16. Among the 128 requests of one index of adapter, at most 16 use adapters of one owner, and exactly 16 use adapters of one common owner, the same for every index.
All inputs are finite; a program needn't handle non-finite values.
Results may differ from a plain program's by a relative error of at most 0.0052.
Values may be sent and summed in bfloat16 or wider, within the bound.
A program may use at most 128 MiB of HBM per device.

v0:
```python
import jax
import jax.numpy as jnp
from jax import lax
from jax.sharding import PartitionSpec as P

adapter_scale = 2.0


def per_device(
    attended, residual, output_matrix, adapter_down_weight, adapter_up_weight, request_adapter_index
):
    groups = lax.axis_size("adapter")
    splits = lax.axis_size("tensor")
    rows_dev, width = attended.shape
    column_slice = width // splits
    adapters_per_device, rank_index, unused_value = adapter_down_weight.shape
    capacity = max(2, rows_dev // 8)
    slots = groups * capacity
    here = lax.axis_index("tensor")
    own_cols = lax.dynamic_slice_in_dim(attended, here * column_slice, column_slice, 1)
    owner = request_adapter_index // adapters_per_device
    local_id = request_adapter_index - owner * adapters_per_device
    hits = (owner[:, None] == jnp.arange(groups, dtype=jnp.int32)[None, :]).astype(jnp.int32)
    before = jnp.cumsum(hits, axis=0) - hits
    position = jnp.sum(before * hits, axis=1)
    target = owner * capacity + position
    placing = jnp.arange(slots, dtype=jnp.int32)[:, None] == target[None, :]
    place_int = placing.astype(jnp.int32)
    send_rows = jnp.dot(placing.astype(jnp.bfloat16), own_cols, preferred_element_type=jnp.float32)
    send_rows = send_rows.astype(jnp.bfloat16).reshape(groups, capacity, column_slice)
    row_numbers = jnp.arange(rows_dev, dtype=jnp.int32)
    send_local = (jnp.sum(place_int * (local_id + 1)[None, :], axis=1) - 1).reshape(
        groups, capacity
    )
    send_row = (jnp.sum(place_int * (row_numbers + 1)[None, :], axis=1) - 1).reshape(
        groups, capacity
    )
    flattened_down = adapter_down_weight.reshape(adapters_per_device * rank_index, column_slice)
    flattened_up = adapter_up_weight.reshape(adapters_per_device * rank_index, column_slice)
    rows_in = lax.all_to_all(send_rows, "adapter", split_axis=0, concat_axis=0, tiled=True)
    local_in = lax.all_to_all(send_local, "adapter", split_axis=0, concat_axis=0, tiled=True)
    row_in = lax.all_to_all(send_row, "adapter", split_axis=0, concat_axis=0, tiled=True)
    count = rows_in.shape[1]
    flat = rows_in.reshape(groups * count, column_slice)
    chosen = (
        local_in.reshape(-1)[:, None] == jnp.arange(adapters_per_device, dtype=jnp.int32)[None, :]
    )
    projected = lax.dot_general(
        flat, flattened_down, (((1,), (1,)), ((), ())), preferred_element_type=jnp.float32
    )
    partial_low = jnp.sum(
        projected.reshape(-1, adapters_per_device, rank_index)
        * chosen.astype(jnp.float32)[:, :, None],
        axis=1,
    )
    lower_bound = lax.psum(partial_low, "tensor").astype(jnp.bfloat16)
    spread_rows = (chosen.astype(jnp.bfloat16)[:, :, None] * lower_bound[:, None, :]).reshape(
        -1, adapters_per_device * rank_index
    )
    lowrank_update = (
        jnp.dot(spread_rows, flattened_up, preferred_element_type=jnp.float32) * adapter_scale
    )
    source = jnp.arange(groups, dtype=jnp.int32)[:, None]
    home = jnp.where(local_in >= 0, source * rows_dev + row_in, -1)
    lowrank_update, home = (
        lowrank_update.astype(jnp.bfloat16).reshape(groups, count, column_slice),
        home,
    )
    homing = (target[:, None] == jnp.arange(slots, dtype=jnp.int32)[None, :]).astype(jnp.bfloat16)
    by_block = lax.all_to_all(attended, "adapter", split_axis=1, concat_axis=0, tiled=True)
    combined = lax.psum_scatter(
        jnp.dot(by_block, output_matrix, preferred_element_type=jnp.float32),
        "adapter",
        scatter_dimension=0,
        tiled=True,
    )
    back = lax.all_to_all(lowrank_update, "adapter", split_axis=0, concat_axis=0, tiled=True)
    combined = combined + jnp.dot(
        homing, back.reshape(slots, column_slice), preferred_element_type=jnp.float32
    )
    return (residual.astype(jnp.float32) + combined).astype(jnp.bfloat16)


def solution(mesh):
    return jax.shard_map(
        per_device,
        mesh=mesh,
        in_specs=(
            P("adapter", None),
            P("adapter", "tensor"),
            P("adapter", "tensor"),
            P("adapter", None, "tensor"),
            P("adapter", None, "tensor"),
            P("adapter"),
        ),
        out_specs=P("adapter", "tensor"),
        check_vma=False,
    )
```

profile of v0, /device:TPU:1, one launch (start us, length us, event | category | flops | bytes accessed | tf_op | source)
XLA Modules:
  0.0 202.7 jit_solution(9446212297403699088)
XLA Ops:
  6.5 0.0 copy-start
  6.5 0.0 reduce-scatter.2.cloned.1.call-start
  6.5 4.2 %copy.14 = bf16[128,8192]{0,1:T(8,128)(2,1)} copy(bf16[128,8192]{1,0:T(8,128)(2,1)} %param.6) | data formatting | bytes 4194304 | tf_op args[0]
  10.8 37.1 %all_to_all.35 = bf16[128,32,256]{0,2,1:T(8,128)(2,1)} all-to-all(bf16[128,32,256]{0,2,1:T(8,128)(2,1)} %bitcast.22), channel_id=1, replica_groups=mesh['adapter'=32,'tensor'=8] {'adapter'}, dimensions={1} | all-to-all | bytes 4194304 | tf_op jit(solution)/shard_map/all_to_all | solution.py:70
  47.9 0.0 copy-start.1
  47.9 4.2 %copy.15 = bf16[32,128,256]{2,1,0:T(8,128)(2,1)} copy(bf16[32,128,256]{1,2,0:T(8,128)(2,1)} %bitcast.21) | data formatting | bytes 4194304 | tf_op jit(solution)/shard_map/all_to_all | solution.py:70
  52.0 0.0 copy-done.1
  52.0 9.6 %fusion.13 = f32[4096,1024]{1,0:T(8,128)} fusion(bf16[4096,256]{1,0:T(8,128)(2,1)} %bitcast.20, bf16[256,1024]{1,0:T(8,128)(2,1)S(1)} %copy-done.1), kind=kOutput, calls=%fused_computation.30 | convolution fusion | flops 2147483648 | bytes 19398656 | tf_op jit(solution)/shard_map/dot_general | solution.py:72
  61.7 0.0 copy-start.3
  61.7 0.0 reduce-scatter.2.cloned.1.call-update
  61.7 0.6 copy-done.3
  62.4 0.1 fusion.9
  62.4 0.2 reduce_window_sum.11
  62.6 0.2 select_reduce_fusion.1
  62.8 0.2 select_reduce_fusion
  63.0 0.7 sub.22
  63.7 3.9 %all-to-all-start.1 = ((s32[32,1,16]{2,1,0:T(1,128)}), s32[32,1,16]{2,1,0:T(1,128)S(1)}, u32[]{:S(2)}, u32[]{:S(2)}) async-start(s32[32,1,16]{2,1,0:T(1,128)} %bitcast.3), calls=%async_computation.2 | async-start | bytes 32768 | tf_op jit(solution)/shard_map/all_to_all | solution.py:41
  67.5 2.4 %convolution_convert_fusion = bf16[512,1024]{1,0:T(8,128)(2,1)} fusion(bf16[128,8192]{1,0:T(8,128)(2,1)} %param.6, s32[]{:T(128)S(6)} %select_n.9, s32[128]{0:T(128)S(1)} %multiply_add_fusion), kind=kOutput, calls=%fused_computation.3 | convolution fusion | flops 134807552 | bytes 1311236 | tf_op jit(solution)/shard_map/dot_general | solution.py:29
  69.9 4.6 %all-to-all-done.1 = s32[32,1,16]{2,1,0:T(1,128)S(1)} async-done(((s32[32,1,16]{2,1,0:T(1,128)}), s32[32,1,16]{2,1,0:T(1,128)S(1)}, u32[]{:S(2)}, u32[]{:S(2)}) %all-to-all-start.1) | async-done | bytes 2080 | tf_op jit(solution)/shard_map/all_to_all | solution.py:41
  74.5 4.2 %all-to-all-start.2 = ((bf16[32,16,1024]{2,1,0:T(8,128)(2,1)}), bf16[32,16,1024]{2,1,0:T(8,128)(2,1)S(1)}, u32[]{:S(2)}, u32[]{:S(2)}) async-start(bf16[32,16,1024]{2,1,0:T(8,128)(2,1)} %bitcast.4), calls=%async_computation.3 | async-start | bytes 2097152 | tf_op jit(solution)/shard_map/all_to_all | solution.py:40
  78.8 0.5 broadcast.72
  79.3 0.7 reduce.3
  80.0 0.1 eq.70
  80.1 16.0 %all-to-all-done.2 = bf16[32,16,1024]{2,1,0:T(8,128)(2,1)S(1)} async-done(((bf16[32,16,1024]{2,1,0:T(8,128)(2,1)}), bf16[32,16,1024]{2,1,0:T(8,128)(2,1)S(1)}, u32[]{:S(2)}, u32[]{:S(2)}) %all-to-all-start.2) | async-done | bytes 1048608 | tf_op jit(solution)/shard_map/all_to_all | solution.py:40
  96.0 3.1 %multiply_reduce_fusion = f32[512,64]{0,1:T(8,128)S(1)} fusion(bf16[512,1024,1]{1,0,2:T(8,128)(2,1)S(1)} %bitcast.24, bf16[16,64,1024]{2,1,0:T(8,128)(2,1)} %param.9, f32[512,16]{0,1:T(8,128)S(1)} %get-tuple-element.8), kind=kOutput, calls=%fused_computation.2 | convolution fusion | flops 1074757632 | bytes 3309568 | tf_op jit(solution)/shard_map/dot_general | solution.py:48
  99.1 27.6 %all-reduce.1 = bf16[512,64]{0,1:T(8,128)(2,1)S(1)} all-reduce(f32[512,64]{0,1:T(8,128)S(1)} %multiply_reduce_fusion), channel_id=1, replica_groups=mesh['adapter'=32,'tensor'=8] {'tensor'}, use_global_device_ids=true, to_apply=%region_5.6 | all-reduce | flops 32768 | bytes 196608 | tf_op jit(solution)/shard_map/psum | solution.py:56
  126.7 0.0 copy-done
  126.7 1.3 fusion
  128.0 0.0 copy-start.2
  128.0 36.3 %all_to_all.36 = bf16[32,16,1024]{2,1,0:T(8,128)(2,1)S(1)} all-to-all(bf16[32,16,1024]{2,1,0:T(8,128)(2,1)S(1)} %bitcast.25), channel_id=1, replica_groups=mesh['adapter'=32,'tensor'=8] {'adapter'}, dimensions={0} | all-to-all | bytes 2097152 | tf_op jit(solution)/shard_map/all_to_all | solution.py:77
  164.3 29.5 %reduce-scatter.2.cloned.1.call-done = f32[128,1024]{1,0:T(8,128)} async-done(((f32[4096,1024]{1,0:T(8,128)}), f32[128,1024]{1,0:T(8,128)}) %reduce-scatter.2.cloned.1.call-update) | async-done | bytes 524304 | tf_op jit(solution)/shard_map/reduce_scatter | solution.py:71
  193.8 0.0 copy-done.2
  193.8 2.1 %fusion.2 = bf16[128,1024]{1,0:T(8,128)(2,1)} fusion(f32[128,1024]{1,0:T(8,128)} %reduce-scatter.2.cloned.1.call-done, bf16[512,1024]{1,0:T(8,128)(2,1)S(1)} %bitcast.23, bf16[128,1024]{1,0:T(8,128)(2,1)S(1)} %copy-done.2, s32[128]{0:T(128)S(1)} %multiply_add_fusion), kind=kOutput, calls=%fused_computation.6 | convolution fusion | flops 134807552 | bytes 2097664 | tf_op jit(solution)/shard_map/dot_general | solution.py:78
  (4 shorter events, 0.0 us)
Async XLA Ops:
  6.5 120.2 %copy-start = (bf16[16,64,1024]{2,1,0:T(8,128)(2,1)S(1)}, bf16[16,64,1024]{2,1,0:T(8,128)(2,1)}, u32[]{:S(2)}) copy-start(bf16[16,64,1024]{2,1,0:T(8,128)(2,1)} %param.10) | copy-start | bytes 6291460
  6.5 187.2 %reduce-scatter.2.cloned.1.call-start = ((), (), s32[]{:S(2)}) async-start(), calls=%async_computation.5 | async-start | bytes 17301504 | tf_op jit(solution)/shard_map/reduce_scatter | solution.py:71
  47.9 4.2 %copy-start.1 = (bf16[256,1024]{1,0:T(8,128)(2,1)S(1)}, bf16[256,1024]{1,0:T(8,128)(2,1)}, u32[]{:S(2)}) copy-start(bf16[256,1024]{1,0:T(8,128)(2,1)} %param.8) | copy-start | bytes 1572868
  61.7 0.7 copy-start.3
  63.7 10.9 %all-to-all-start.1 = ((s32[32,1,16]{2,1,0:T(1,128)}), s32[32,1,16]{2,1,0:T(1,128)S(1)}, u32[]{:S(2)}, u32[]{:S(2)}) async-start(s32[32,1,16]{2,1,0:T(1,128)} %bitcast.3), calls=%async_computation.2 | async-start | bytes 32768 | tf_op jit(solution)/shard_map/all_to_all | solution.py:41
  74.5 21.5 %all-to-all-start.2 = ((bf16[32,16,1024]{2,1,0:T(8,128)(2,1)}), bf16[32,16,1024]{2,1,0:T(8,128)(2,1)S(1)}, u32[]{:S(2)}, u32[]{:S(2)}) async-start(bf16[32,16,1024]{2,1,0:T(8,128)(2,1)} %bitcast.4), calls=%async_computation.3 | async-start | bytes 2097152 | tf_op jit(solution)/shard_map/all_to_all | solution.py:40
  128.0 65.8 %copy-start.2 = (bf16[128,1024]{1,0:T(8,128)(2,1)S(1)}, bf16[128,1024]{1,0:T(8,128)(2,1)}, u32[]{:S(2)}) copy-start(bf16[128,1024]{1,0:T(8,128)(2,1)} %param.7) | copy-start | bytes 786436
Sparse Core Ops, SparseCore 0:
  61.8 131.8 reduce-scatter.1
where the time goes:
time: 204 us; the launch traced here: 203 us
  blocking collectives  101 us (50%)
  waiting for transfers between devices  50.1 us (25%)
  matrix products  18.5 us (9%)
  between operations  13.5 us (7%)
  local copies, waits for them, and re-layouts  10.3 us (5%)
  starting transfers between devices  8.11 us (4%)
    all_to_all x1, blocking collectives, per_device(): lax.all_to_all(attended, 'adapter', split_axis=1, concat_axis=0, tiled=True)  37.1 us
    all_to_all x1, blocking collectives, per_device(): lax.all_to_all(lowrank_update, 'adapter', split_axis=0, concat_axis=0, ti...  36.3 us
    reduce_scatter x1, waiting for transfers between devices, per_device(): lax.psum_scatter(jnp.dot(by_block, output_matrix, preferred_element_type=...  29.5 us
    psum x1, blocking collectives, per_device(): lower_bound = lax.psum(partial_low, 'tensor').astype(jnp.bfloat16)  27.6 us
    all_to_all x1, waiting for transfers between devices, per_device(): lax.all_to_all(send_rows, 'adapter', split_axis=0, concat_axis=0, tiled=T...  16 us
    dot_general x1, matrix products, per_device(): jnp.dot(by_block, output_matrix, preferred_element_type=jnp.float32)  9.65 us
    unnamed x9, local copies, waits for them, and re-layouts  4.87 us
    all_to_all x1, waiting for transfers between devices, per_device(): lax.all_to_all(send_local, 'adapter', split_axis=0, concat_axis=0, tiled=...  4.59 us
  transfers between devices with their start and end apart: 3, of which 3 were waited for; matrix products, arithmetic and copies ran while one was open for 5% of the time, Pallas kernels for 0%

commit v1 on v0

v1 whole, which is shorter than its diff:
```python
import functools

import jax
import jax.numpy as jnp
from jax import lax
from jax.experimental import pallas as pl
from jax.experimental.pallas import tpu as pltpu
from jax.sharding import PartitionSpec as P

adapter_scale = 2.0
NY, NX, NC = 4, 4, 2
GROUPS = NY * NX * NC
CAP = 16
META = 128
MESH = pl.DeviceIdType.MESH
f32, bf16, i32 = jnp.float32, jnp.bfloat16, jnp.int32


def iota(shape, dim):
    return lax.broadcasted_iota(i32, shape, dim)


def kernel(
    nz, idx_ref, att, res_hbm, w_hbm, down_hbm, up_hbm, out_ref,
    xz, res, down, up, fwd, got, low_own, low_in, low_sum, low_all, spread, delta, back,
    xb, wg, keep, sib_out, sib_in, sum_out, sum_in,
    load_sem, fs, fr, bs, br, ls, lr, gs, gr, xs, xr, es, er, ws, wr, ps, pr, rs, rr,
):
    me = lax.axis_index("adapter")
    z = lax.axis_index("tensor")
    core = lax.rem(me, NC)
    x = lax.rem(lax.div(me, NC), NX)
    y = lax.div(me, NC * NX)
    par = lax.rem(z, 2)
    rows, cols = out_ref.shape
    slots = GROUPS * CAP
    kcols = xb.shape[-1]
    quarter = rows // 4
    wblk = w_hbm.shape[0]

    def dev(yy, xx, cc):
        return (yy * NX + xx) * NC + cc

    def remote(src, dst, ssem, rsem, a, t):
        return pltpu.make_async_remote_copy(
            src_ref=src, dst_ref=dst, send_sem=ssem, recv_sem=rsem,
            device_id=(a, t), device_id_type=MESH)

    load_x = pltpu.make_async_copy(
        att.at[:, pl.ds(pl.multiple_of(z * cols, cols), cols)], xz, load_sem.at[0])
    load_x.start()
    load_down = pltpu.make_async_copy(down_hbm, down, load_sem.at[1])
    load_down.start()
    load_up = pltpu.make_async_copy(up_hbm, up, load_sem.at[2])
    load_up.start()
    load_res = pltpu.make_async_copy(res_hbm, res, load_sem.at[3])
    load_res.start()

    barrier = pltpu.get_barrier_semaphore()

    def greet(d, _):
        pl.semaphore_signal(barrier, inc=1, device_id=(lax.rem(me + d, GROUPS), z),
                            device_id_type=MESH)
        return 0

    lax.fori_loop(1, GROUPS, greet, 0)

    def greet_z(d, _):
        pl.semaphore_signal(barrier, inc=1, device_id=(me, lax.rem(z + d, nz)),
                            device_id_type=MESH)
        return 0

    lax.fori_loop(1, nz, greet_z, 0)

    ids = idx_ref[...]
    owner = lax.shift_right_logical(ids, 4)
    local = lax.bitwise_and(ids, CAP - 1)
    hits = (iota((GROUPS, rows), 0) == owner).astype(bf16)
    earlier = (iota((rows, rows), 0) < iota((rows, rows), 1)).astype(bf16)
    before = jnp.dot(hits, earlier, preferred_element_type=f32)
    position = jnp.sum(before * hits.astype(f32), axis=0, keepdims=True)
    target = owner.astype(f32) * CAP + position
    eye = iota((rows, rows), 0) == iota((rows, rows), 1)
    target_col = jnp.sum(jnp.where(eye, target, 0.0), axis=1, keepdims=True)
    local_col = jnp.sum(jnp.where(eye, local.astype(f32), 0.0), axis=1, keepdims=True)
    placing = (iota((slots, rows), 0) == target.astype(i32)).astype(bf16)

    load_x.wait()
    fwd[:, :cols] = jnp.dot(placing, xz[...], preferred_element_type=f32).astype(bf16)
    fwd[:, cols:] = jnp.dot(
        placing, jnp.broadcast_to(local_col, (rows, META)).astype(bf16),
        preferred_element_type=f32).astype(bf16)

    pl.semaphore_wait(barrier, GROUPS - 1 + nz - 1)

    def block(ref, i):
        return ref.at[pl.ds(pl.multiple_of(i * CAP, CAP), CAP), :]

    def send_fwd(d, _):
        to = lax.rem(me + d, GROUPS)
        remote(block(fwd, to), block(got, me), fs.at[to], fr.at[me], to, z).start()
        return 0

    lax.fori_loop(1, GROUPS, send_fwd, 0)
    pltpu.make_async_copy(block(fwd, me), block(got, me), fr.at[me]).start()

    chunk = (par, 3 - par)

    def x_copy(part, dy, dc):
        yd = lax.rem(y + dy, NY)
        cd = lax.rem(core + dc, NC)
        src = att.at[pl.ds(pl.multiple_of(chunk[part] * quarter, quarter), quarter),
                     pl.ds(pl.multiple_of((yd * NC + cd) * kcols, kcols), kcols)]
        dst = xb.at[chunk[part], dc, y]
        if dy == 0 and dc == 0:
            return pltpu.make_async_copy(src, dst, xr.at[part, dc, y])
        return remote(src, dst, xs.at[part, dc, dy], xr.at[part, dc, y], dev(yd, x, cd), z)

    for part in range(2):
        for dy in range(NY):
            for dc in range(NC):
                x_copy(part, dy, dc).start()

    half = lax.div(x, 2)
    spot = lax.rem(x, 2) * NC + core

    def w_copy(dx):
        return remote(w_hbm, wg.at[pl.ds(pl.multiple_of(spot * wblk, wblk), wblk), :],
                      ws.at[dx], wr.at[spot], dev(y, lax.rem(x + dx, NX), half), z)

    for dx in (1, 3, 2):
        w_copy(dx).start()

    @pl.when(half == core)
    def _():
        pltpu.make_async_copy(
            w_hbm, wg.at[pl.ds(pl.multiple_of(spot * wblk, wblk), wblk), :], wr.at[spot]).start()

    @pl.when(half != core)
    def _():
        w_copy(0).start()

    def e_copy(part, rel, yy):
        if part == 0:
            to = z + 1 - 2 * par
        else:
            to = lax.rem(z + nz - 1 + 2 * par, nz)
        ref = xb.at[chunk[part], rel, yy]
        return remote(ref, ref, es.at[part, rel, yy], er.at[part, rel, yy], me, to)

    def x_arrived(part, rel, yy):
        ref = xb.at[chunk[part], rel, yy]
        pltpu.make_async_copy(ref, ref, xr.at[part, rel, yy]).wait()

    def forward(i, _):
        yy = lax.rem(i, NY)
        rel = lax.div(i, NY)
        for part in range(2):
            x_arrived(part, rel, yy)
            e_copy(part, rel, yy).start()
        return 0

    lax.fori_loop(0, NY * NC, forward, 0)

    def got_fwd(s, _):
        pltpu.make_async_copy(block(got, s), block(got, s), fr.at[s]).wait()
        return 0

    lax.fori_loop(0, GROUPS, got_fwd, 0)
    load_down.wait()
    lane = iota((slots, 128), 1)
    mine = got[:, cols:].astype(f32) - (lane >= 64).astype(f32)
    acc = jnp.zeros((slots, 128), f32)
    for t in range(4):
        projected = lax.dot_general(
            got[:, :cols], down[t * 256:(t + 1) * 256, :], (((1,), (1,)), ((), ())),
            preferred_element_type=f32)
        for u in range(2):
            acc += jnp.where(mine == 2.0 * (2 * t + u), projected[:, u * 128:(u + 1) * 128], 0.0)
    acc = acc + pltpu.roll(acc, 64, 1)
    first = iota((slots // 2, 128), 1) < 64
    low_own[...] = jnp.where(first, acc[:slots // 2], acc[slots // 2:]).reshape(low_own.shape)

    def low_send(d, _):
        to = lax.rem(z + d, nz)
        remote(low_own.at[to], low_in.at[z], ls.at[to], lr.at[z], me, to).start()
        return 0

    lax.fori_loop(1, nz, low_send, 0)

    def w_arrived(p, _):
        ref = wg.at[pl.ds(pl.multiple_of(p * wblk, wblk), wblk), :]
        pltpu.make_async_copy(ref, ref, wr.at[p]).wait()
        return 0

    lax.fori_loop(0, 4, w_arrived, 0)

    def base(k):
        place = pl.ds(pl.multiple_of(k * quarter, quarter), quarter)
        tile = min(256, cols)

        def one(n, _):
            at = pl.ds(pl.multiple_of(n * tile, tile), tile)
            r = jnp.dot(xb[k].reshape(NC * NY * quarter, kcols), wg[:, at],
                        preferred_element_type=f32)
            r = r.reshape(NC, NY, quarter, tile)
            keep[:, place, at] = r[0]
            sib_out[:, place, at] = r[1].astype(bf16)
            return 0

        lax.fori_loop(0, cols // tile, one, 0)

    base(chunk[0])
    base(chunk[1])

    def low_got(d, total):
        s = lax.rem(z + d, nz)
        pltpu.make_async_copy(low_in.at[s], low_in.at[s], lr.at[s]).wait()
        return total + low_in[s]

    low_sum[...] = lax.fori_loop(1, nz, low_got, low_own[z]).astype(bf16)

    def low_spread(d, _):
        to = lax.rem(z + d, nz)
        remote(low_sum, low_all.at[z], gs.at[to], gr.at[z], me, to).start()
        return 0

    lax.fori_loop(1, nz, low_spread, 0)
    low_all[z] = low_sum[...]

    other = (1 - par, 2 + par)

    def e_arrived(i, _):
        yy = lax.rem(i, NY)
        rel = lax.div(i, NY)
        for part in range(2):
            ref = xb.at[other[part], rel, yy]
            pltpu.make_async_copy(ref, ref, er.at[part, rel, yy]).wait()
        return 0

    lax.fori_loop(0, NY * NC, e_arrived, 0)
    base(other[0])
    base(other[1])

    def pair_copy(yy):
        return remote(sib_out.at[yy], sib_in.at[yy], ps.at[yy], pr.at[yy],
                      dev(y, x, 1 - core), z)

    for dy in (2, 1, 3, 0):
        pair_copy(lax.rem(y + dy, NY)).start()

    def low_here(d, _):
        s = lax.rem(z + d, nz)
        pltpu.make_async_copy(low_all.at[s], low_all.at[s], gr.at[s]).wait()
        return 0

    lax.fori_loop(1, nz, low_here, 0)
    load_up.wait()
    packed = low_all[...].reshape(slots // 2, 128).astype(f32)
    turned = pltpu.roll(packed, 64, 1)
    low = jnp.concatenate(
        [jnp.where(first, packed, turned), jnp.where(first, turned, packed)], axis=0)
    for j in range(8):
        spread[:, j * 128:(j + 1) * 128] = jnp.where(mine == 2.0 * j, low, 0.0).astype(bf16)
    tile = min(256, cols)

    def up_tile(n, _):
        at = pl.ds(pl.multiple_of(n * tile, tile), tile)
        delta[:, at] = (jnp.dot(spread[...], up[:, at], preferred_element_type=f32)
                        * adapter_scale).astype(bf16)
        return 0

    lax.fori_loop(0, cols // tile, up_tile, 0)

    def send_back(d, _):
        to = lax.rem(me + d, GROUPS)
        remote(block(delta, to), block(back, me), bs.at[to], br.at[me], to, z).start()
        return 0

    lax.fori_loop(1, GROUPS, send_back, 0)
    pltpu.make_async_copy(block(delta, me), block(back, me), br.at[me]).start()

    def sum_copy(dy):
        yd = lax.rem(y + dy, NY)
        return remote(sum_out.at[dy], sum_in.at[dy], rs.at[dy], rr.at[dy], dev(yd, x, core), z)

    for dy in (2, 1, 3, 0):
        yd = lax.rem(y + dy, NY)
        pltpu.make_async_copy(sib_in.at[yd], sib_in.at[yd], pr.at[yd]).wait()
        if dy == 0:
            keep[yd] = keep[yd] + sib_in[yd].astype(f32)
        else:
            sum_out[dy] = (keep[yd] + sib_in[yd].astype(f32)).astype(bf16)
            sum_copy(dy).start()

    load_res.wait()
    for dy in (1, 3, 2):
        pltpu.make_async_copy(sum_in.at[dy], sum_in.at[dy], rr.at[dy]).wait()
    total = (res[...].astype(f32) + keep[y] + sum_in[1].astype(f32) + sum_in[2].astype(f32)
             + sum_in[3].astype(f32))
    homing = (iota((rows, slots), 1) == target_col.astype(i32)).astype(bf16)

    def got_back(s, _):
        pltpu.make_async_copy(block(back, s), block(back, s), br.at[s]).wait()
        return 0

    lax.fori_loop(0, GROUPS, got_back, 0)
    total = total + jnp.dot(homing, back[...], preferred_element_type=f32)
    out_ref[...] = total.astype(bf16)

    def sent(d, _):
        to = lax.rem(me + d, GROUPS)
        remote(block(fwd, to), block(got, me), fs.at[to], fr.at[me], to, z).wait_send()
        remote(block(delta, to), block(back, me), bs.at[to], br.at[me], to, z).wait_send()
        return 0

    lax.fori_loop(1, GROUPS, sent, 0)

    def sent_z(d, _):
        to = lax.rem(z + d, nz)
        remote(low_own.at[to], low_in.at[z], ls.at[to], lr.at[z], me, to).wait_send()
        remote(low_sum, low_all.at[z], gs.at[to], gr.at[z], me, to).wait_send()
        return 0

    lax.fori_loop(1, nz, sent_z, 0)
    for part in range(2):
        for dy in range(NY):
            for dc in range(NC):
                if dy or dc:
                    x_copy(part, dy, dc).wait_send()
                e_copy(part, dc, dy).wait_send()
    for dx in (1, 2, 3):
        w_copy(dx).wait_send()
        sum_copy(dx).wait_send()

    @pl.when(half != core)
    def _():
        w_copy(0).wait_send()

    for dy in range(NY):
        pair_copy(dy).wait_send()


def per_device(
    attended, residual, output_matrix, adapter_down_weight, adapter_up_weight, request_adapter_index
):
    nz = lax.axis_size("tensor")
    rows, width = attended.shape
    cols = width // nz
    kcols = width // (NY * NC)
    adapters, rank, unused_value = adapter_down_weight.shape
    slots = GROUPS * CAP
    wide = adapters * rank
    quarter = rows // 4
    dma = pltpu.SemaphoreType.DMA
    anyspace = pl.BlockSpec(memory_space=pl.ANY)
    vmem = pl.BlockSpec(memory_space=pltpu.VMEM)
    return pl.pallas_call(
        functools.partial(kernel, nz),
        out_shape=jax.ShapeDtypeStruct((rows, cols), bf16),
        in_specs=[vmem] + [anyspace] * 5,
        out_specs=vmem,
        scratch_shapes=[
            pltpu.VMEM((rows, cols), bf16),
            pltpu.VMEM((rows, cols), bf16),
            pltpu.VMEM((wide, cols), bf16),
            pltpu.VMEM((wide, cols), bf16),
            pltpu.VMEM((slots, cols + META), bf16),
            pltpu.VMEM((slots, cols + META), bf16),
            pltpu.VMEM((nz, slots // 2 // nz, 128), f32),
            pltpu.VMEM((nz, slots // 2 // nz, 128), f32),
            pltpu.VMEM((slots // 2 // nz, 128), bf16),
            pltpu.VMEM((nz, slots // 2 // nz, 128), bf16),
            pltpu.VMEM((slots, wide), bf16),
            pltpu.VMEM((slots, cols), bf16),
            pltpu.VMEM((slots, cols), bf16),
            pltpu.VMEM((4, NC, NY, quarter, kcols), bf16),
            pltpu.VMEM((kcols, cols), bf16),
            pltpu.VMEM((NY, rows, cols), f32),
            pltpu.VMEM((NY, rows, cols), bf16),
            pltpu.VMEM((NY, rows, cols), bf16),
            pltpu.VMEM((NY, rows, cols), bf16),
            pltpu.VMEM((NY, rows, cols), bf16),
            dma((4,)),
            dma((GROUPS,)), dma((GROUPS,)),
            dma((GROUPS,)), dma((GROUPS,)),
            dma((nz,)), dma((nz,)),
            dma((nz,)), dma((nz,)),
            dma((2, NC, NY)), dma((2, NC, NY)),
            dma((2, NC, NY)), dma((2, NC, NY)),
            dma((4,)), dma((4,)),
            dma((NY,)), dma((NY,)),
            dma((NY,)), dma((NY,)),
        ],
        compiler_params=pltpu.CompilerParams(
            collective_id=0, has_side_effects=True, vmem_limit_bytes=60 * 1024 * 1024),
    )(
        request_adapter_index.reshape(1, rows), attended, residual, output_matrix,
        adapter_down_weight.reshape(wide, cols), adapter_up_weight.reshape(wide, cols),
    )


def solution(mesh):
    return jax.shard_map(
        per_device,
        mesh=mesh,
        in_specs=(
            P("adapter", None),
            P("adapter", "tensor"),
            P("adapter", "tensor"),
            P("adapter", None, "tensor"),
            P("adapter", None, "tensor"),
            P("adapter"),
        ),
        out_specs=P("adapter", "tensor"),
        check_vma=False,
    )
```

time: 204 us -> 89.7 us (0.44)
  blocking collectives: 101 us -> 0 us
  Pallas kernels: 0 us -> 87.9 us
  waiting for transfers between devices: 50.1 us -> 0 us
  matrix products: 18.5 us -> 0 us
  between operations: 13.5 us -> 0.01 us
  local copies, waits for them, and re-layouts: 10.3 us -> 1.67 us
  starting transfers between devices: 8.11 us -> 0 us
    pallas_call x0 -> x1, Pallas kernels: none -> 87.9 us  [per_device(): pl.pallas_call(functools.partial(kernel, nz), out_shape=jax.ShapeDtypeStr...]
    all_to_all x2 -> x0, blocking collectives: 73.4 us -> none  [the longest x1 37.1 us: per_device(): lax.all_to_all(attended, 'adapter', split_axis=1, concat_axis=0, tiled=True)]
    reduce_scatter x1 -> x0, waiting for transfers between devices: 29.5 us -> none  [per_device(): lax.psum_scatter(jnp.dot(by_block, output_matrix, preferred_element_type=...]
    psum x1 -> x0, blocking collectives: 27.6 us -> none  [per_device(): lower_bound = lax.psum(partial_low, 'tensor').astype(jnp.bfloat16)]
    all_to_all x2 -> x0, waiting for transfers between devices: 20.6 us -> none  [the longest x1 16 us: per_device(): lax.all_to_all(send_rows, 'adapter', split_axis=0, concat_axis=0, tiled=T...]
    dot_general x5 -> x0, matrix products: 18.5 us -> none  [the longest x1 9.65 us: per_device(): jnp.dot(by_block, output_matrix, preferred_element_type=jnp.float32)]
    all_to_all x2 -> x0, starting transfers between devices: 8.11 us -> none  [the longest x1 4.24 us: per_device(): lax.all_to_all(send_rows, 'adapter', split_axis=0, concat_axis=0, tiled=T...]
    all_to_all x2 -> x0, local copies, waits for them, and re-layouts: 4.67 us -> none  [the longest x1 4.16 us: per_device(): lax.all_to_all(attended, 'adapter', split_axis=1, concat_axis=0, tiled=True)]
  transfers between devices with their start and end apart: 3 -> 0, of which waited for: 3 -> 0; matrix products, arithmetic and copies ran while one was open for 5% -> 0% of each run, Pallas kernels for 0% -> 0%
where the time goes in v1:
time: 89.7 us; the launch traced here: 89.6 us
  Pallas kernels  87.9 us (98%)
  local copies, waits for them, and re-layouts  1.67 us (2%)
    pallas_call x1, Pallas kernels, per_device(): pl.pallas_call(functools.partial(kernel, nz), out_shape=jax.ShapeDtypeStr...  87.9 us

profile of v1, /device:TPU:1, one launch (start us, length us, event | category | flops | bytes accessed | tf_op | source)
XLA Modules:
  0.0 89.6 jit_solution(18178452457972645636)
XLA Ops:
  0.0 87.9 %shard_map.64 = bf16[128,1024]{1,0:T(8,128)(2,1)} custom-call(s32[1,128]{1,0:T(1,128)} %bitcast.5, bf16[128,8192]{1,0:T(8,128)(2,1)} %att.1, bf16[128,1024]{1,0:T(8,128)(2,1)} %res_hbm.1, bf16[256,1024]{1,0:T(8,128)(2,1)} %w_hbm.1, bf16[1024,1024]{1,0:T(8,128)(2,1)} %bitcast.3, bf16[1024,1024]{1,0:T(8,128)(2,1)} %bitcast.4), custom_call_target="tpu_custom_call" | custom-call | tf_op jit(solution)/shard_map/pallas_call | solution.py:358
  87.9 1.7 %copy.8 = bf16[128,1024]{1,0:T(8,128)(2,1)} copy(bf16[128,1024]{1,0:T(8,128)(2,1)} %shard_map.64) | data formatting | bytes 524288

commit v2 on v1

--- a/solution.py
+++ b/solution.py
@@ -13,6 +13,9 @@
 CAP = 16
 META = 128
 MESH = pl.DeviceIdType.MESH
+FAR_FIRST = sorted(
+    ((dy, dx, dc) for dy in range(NY) for dx in range(NX) for dc in range(NC) if dy or dx or dc),
+    key=lambda o: -min(o[0], NY - o[0]) - min(o[1], NX - o[1]))
 f32, bf16, i32 = jnp.float32, jnp.bfloat16, jnp.int32
 
 
@@ -24,14 +27,14 @@
     nz, idx_ref, att, res_hbm, w_hbm, down_hbm, up_hbm, out_ref,
     xz, res, down, up, fwd, got, low_own, low_in, low_sum, low_all, spread, delta, back,
     xb, wg, keep, sib_out, sib_in, sum_out, sum_in,
-    load_sem, fs, fr, bs, br, ls, lr, gs, gr, xs, xr, es, er, ws, wr, ps, pr, rs, rr,
+    load_sem, fs, fr, bs, br, ls, lr, gs, gr, xs, xr, es, er, hs, hr, ws, wr, vs, ps, pr, rs, rr,
 ):
     me = lax.axis_index("adapter")
     z = lax.axis_index("tensor")
     core = lax.rem(me, NC)
     x = lax.rem(lax.div(me, NC), NX)
     y = lax.div(me, NC * NX)
-    par = lax.rem(z, 2)
+    mine_q = lax.rem(z, 4)
     rows, cols = out_ref.shape
     slots = GROUPS * CAP
     kcols = xb.shape[-1]
@@ -96,71 +99,99 @@
     def block(ref, i):
         return ref.at[pl.ds(pl.multiple_of(i * CAP, CAP), CAP), :]
 
-    def send_fwd(d, _):
-        to = lax.rem(me + d, GROUPS)
-        remote(block(fwd, to), block(got, me), fs.at[to], fr.at[me], to, z).start()
-        return 0
-
-    lax.fori_loop(1, GROUPS, send_fwd, 0)
-    pltpu.make_async_copy(block(fwd, me), block(got, me), fr.at[me]).start()
-
-    chunk = (par, 3 - par)
-
-    def x_copy(part, dy, dc):
+    def fwd_copy(to):
+        return remote(block(fwd, to), block(got, me), fs.at[to], fr.at[me], to, z)
+
+    def x_copy(dy, dc):
         yd = lax.rem(y + dy, NY)
         cd = lax.rem(core + dc, NC)
-        src = att.at[pl.ds(pl.multiple_of(chunk[part] * quarter, quarter), quarter),
+        src = att.at[pl.ds(pl.multiple_of(mine_q * quarter, quarter), quarter),
                      pl.ds(pl.multiple_of((yd * NC + cd) * kcols, kcols), kcols)]
-        dst = xb.at[chunk[part], dc, y]
+        dst = xb.at[mine_q, dc, y]
         if dy == 0 and dc == 0:
-            return pltpu.make_async_copy(src, dst, xr.at[part, dc, y])
-        return remote(src, dst, xs.at[part, dc, dy], xr.at[part, dc, y], dev(yd, x, cd), z)
-
-    for part in range(2):
-        for dy in range(NY):
+            return pltpu.make_async_copy(src, dst, xr.at[dc, y])
+        return remote(src, dst, xs.at[dc, dy], xr.at[dc, y], dev(yd, x, cd), z)
+
+    def send_x():
+        for dy in (2, 1, 3, 0):
             for dc in range(NC):
-                x_copy(part, dy, dc).start()
+                x_copy(dy, dc).start()
+
+    send_x()
+    for dy, dx, dc in FAR_FIRST:
+        fwd_copy(dev(lax.rem(y + dy, NY), lax.rem(x + dx, NX), lax.rem(core + dc, NC))).start()
+    pltpu.make_async_copy(block(fwd, me), block(got, me), fr.at[me]).start()
 
     half = lax.div(x, 2)
     spot = lax.rem(x, 2) * NC + core
-
-    def w_copy(dx):
-        return remote(w_hbm, wg.at[pl.ds(pl.multiple_of(spot * wblk, wblk), wblk), :],
-                      ws.at[dx], wr.at[spot], dev(y, lax.rem(x + dx, NX), half), z)
-
-    for dx in (1, 3, 2):
-        w_copy(dx).start()
-
-    @pl.when(half == core)
-    def _():
-        pltpu.make_async_copy(
-            w_hbm, wg.at[pl.ds(pl.multiple_of(spot * wblk, wblk), wblk), :], wr.at[spot]).start()
-
-    @pl.when(half != core)
-    def _():
-        w_copy(0).start()
-
-    def e_copy(part, rel, yy):
-        if part == 0:
-            to = z + 1 - 2 * par
-        else:
-            to = lax.rem(z + nz - 1 + 2 * par, nz)
-        ref = xb.at[chunk[part], rel, yy]
-        return remote(ref, ref, es.at[part, rel, yy], er.at[part, rel, yy], me, to)
-
-    def x_arrived(part, rel, yy):
-        ref = xb.at[chunk[part], rel, yy]
-        pltpu.make_async_copy(ref, ref, xr.at[part, rel, yy]).wait()
-
-    def forward(i, _):
+    hblk = wblk // 2
+
+    def w_part(p, h):
+        return wg.at[pl.ds(pl.multiple_of(p * wblk + h * hblk, hblk), hblk), :]
+
+    def w_copy(dx, h):
+        return remote(w_hbm.at[pl.ds(h * hblk, hblk), :], w_part(spot, h), ws.at[dx, h],
+                      wr.at[spot, h], dev(y, lax.rem(x + dx, NX), half), z)
+
+    def send_w():
+        for i in range(2):
+            w_copy(1, i).start()
+            w_copy(3, 1 - i).start()
+
+        @pl.when(half == core)
+        def _():
+            for h in range(2):
+                pltpu.make_async_copy(w_hbm.at[pl.ds(h * hblk, hblk), :], w_part(spot, h),
+                                      wr.at[spot, h]).start()
+
+        @pl.when(half != core)
+        def _():
+            for h in range(2):
+                w_copy(0, h).start()
+
+    ahead = lax.rem(x - 2 * core + NX, NX)
+    near = lax.rem(ahead + 1, 2)
+    side = 1 - lax.rem(lax.div(ahead + 1, 2), 2)
+
+    def w_pass(c):
+        part = w_part(near * NC + c, side)
+        return remote(part, part, vs.at[c], wr.at[near * NC + c, side],
+                      dev(y, lax.rem(x + 1 + 2 * side, NX), core), z)
+
+    def w_arrived(p, h):
+        pltpu.make_async_copy(w_part(p, h), w_part(p, h), wr.at[p, h]).wait()
+
+    right, left = lax.rem(z + 1, nz), lax.rem(z + nz - 1, nz)
+    left_q, right_q, far_q = lax.rem(mine_q + 3, 4), lax.rem(mine_q + 1, 4), lax.rem(mine_q + 2, 4)
+
+    def e_copy(way, rel, yy):
+        ref = xb.at[mine_q, rel, yy]
+        return remote(ref, ref, es.at[way, rel, yy], er.at[way, rel, yy], me, (right, left)[way])
+
+    def h_copy(way, yy):
+        ref = xb.at[(left_q, right_q)[way], way, yy]
+        return remote(ref, ref, hs.at[way, yy], hr.at[way, yy], me, (right, left)[way])
+
+    def arrived(q, rel, yy, sem):
+        ref = xb.at[q, rel, yy]
+        pltpu.make_async_copy(ref, ref, sem).wait()
+
+    def share(i, _):
         yy = lax.rem(i, NY)
         rel = lax.div(i, NY)
-        for part in range(2):
-            x_arrived(part, rel, yy)
-            e_copy(part, rel, yy).start()
-        return 0
-
-    lax.fori_loop(0, NY * NC, forward, 0)
+        arrived(mine_q, rel, yy, xr.at[rel, yy])
+        e_copy(0, rel, yy).start()
+        e_copy(1, rel, yy).start()
+        return 0
+
+    def share_on(yy, _):
+        for way in range(2):
+            arrived((left_q, right_q)[way], way, yy, er.at[way, way, yy])
+            h_copy(way, yy).start()
+        return 0
+
+    lax.fori_loop(0, NY * NC, share, 0)
+    send_w()
 
     def got_fwd(s, _):
         pltpu.make_async_copy(block(got, s), block(got, s), fr.at[s]).wait()
@@ -188,13 +219,6 @@
 
     lax.fori_loop(1, nz, low_send, 0)
 
-    def w_arrived(p, _):
-        ref = wg.at[pl.ds(pl.multiple_of(p * wblk, wblk), wblk), :]
-        pltpu.make_async_copy(ref, ref, wr.at[p]).wait()
-        return 0
-
-    lax.fori_loop(0, 4, w_arrived, 0)
-
     def base(k):
         place = pl.ds(pl.multiple_of(k * quarter, quarter), quarter)
         tile = min(256, cols)
@@ -210,8 +234,9 @@
 
         lax.fori_loop(0, cols // tile, one, 0)
 
-    base(chunk[0])
-    base(chunk[1])
+    for c in range(NC):
+        w_arrived(near * NC + c, side)
+        w_pass(c).start()
 
     def low_got(d, total):
         s = lax.rem(z + d, nz)
@@ -228,19 +253,60 @@
     lax.fori_loop(1, nz, low_spread, 0)
     low_all[z] = low_sum[...]
 
-    other = (1 - par, 2 + par)
-
-    def e_arrived(i, _):
-        yy = lax.rem(i, NY)
-        rel = lax.div(i, NY)
-        for part in range(2):
-            ref = xb.at[other[part], rel, yy]
-            pltpu.make_async_copy(ref, ref, er.at[part, rel, yy]).wait()
-        return 0
-
-    lax.fori_loop(0, NY * NC, e_arrived, 0)
-    base(other[0])
-    base(other[1])
+    def up_and_back():
+        def low_here(d, _):
+            s = lax.rem(z + d, nz)
+            pltpu.make_async_copy(low_all.at[s], low_all.at[s], gr.at[s]).wait()
+            return 0
+
+        lax.fori_loop(1, nz, low_here, 0)
+        load_up.wait()
+        packed = low_all[...].reshape(slots // 2, 128).astype(f32)
+        turned = pltpu.roll(packed, 64, 1)
+        low = jnp.concatenate(
+            [jnp.where(first, packed, turned), jnp.where(first, turned, packed)], axis=0)
+        for j in range(8):
+            spread[:, j * 128:(j + 1) * 128] = jnp.where(mine == 2.0 * j, low, 0.0).astype(bf16)
+        tile = min(256, cols)
+
+        def up_tile(n, _):
+            at = pl.ds(pl.multiple_of(n * tile, tile), tile)
+            delta[:, at] = (jnp.dot(spread[...], up[:, at], preferred_element_type=f32)
+                            * adapter_scale).astype(bf16)
+            return 0
+
+        lax.fori_loop(0, cols // tile, up_tile, 0)
+
+        for dy, dx, dc in FAR_FIRST:
+            to = dev(lax.rem(y + dy, NY), lax.rem(x + dx, NX), lax.rem(core + dc, NC))
+            remote(block(delta, to), block(back, me), bs.at[to], br.at[me], to, z).start()
+        pltpu.make_async_copy(block(delta, me), block(back, me), br.at[me]).start()
+
+    up_and_back()
+    lax.fori_loop(0, NY, share_on, 0)
+
+    for c in range(NC):
+        w_arrived(near * NC + c, 1 - side)
+        w_arrived((1 - near) * NC + c, 0)
+        w_arrived((1 - near) * NC + c, 1)
+    base(mine_q)
+
+    def from_sides(yy, _):
+        arrived(left_q, 1, yy, er.at[0, 1, yy])
+        arrived(right_q, 0, yy, er.at[1, 0, yy])
+        return 0
+
+    lax.fori_loop(0, NY, from_sides, 0)
+    base(left_q)
+    base(right_q)
+
+    def from_far(yy, _):
+        for way in range(2):
+            arrived(far_q, way, yy, hr.at[way, yy])
+        return 0
+
+    lax.fori_loop(0, NY, from_far, 0)
+    base(far_q)
 
     def pair_copy(yy):
         return remote(sib_out.at[yy], sib_in.at[yy], ps.at[yy], pr.at[yy],
@@ -248,37 +314,6 @@
 
     for dy in (2, 1, 3, 0):
         pair_copy(lax.rem(y + dy, NY)).start()
-
-    def low_here(d, _):
-        s = lax.rem(z + d, nz)
-        pltpu.make_async_copy(low_all.at[s], low_all.at[s], gr.at[s]).wait()
-        return 0
-
-    lax.fori_loop(1, nz, low_here, 0)
-    load_up.wait()
-    packed = low_all[...].reshape(slots // 2, 128).astype(f32)
-    turned = pltpu.roll(packed, 64, 1)
-    low = jnp.concatenate(
-        [jnp.where(first, packed, turned), jnp.where(first, turned, packed)], axis=0)
-    for j in range(8):
-        spread[:, j * 128:(j + 1) * 128] = jnp.where(mine == 2.0 * j, low, 0.0).astype(bf16)
-    tile = min(256, cols)
-
-    def up_tile(n, _):
-        at = pl.ds(pl.multiple_of(n * tile, tile), tile)
-        delta[:, at] = (jnp.dot(spread[...], up[:, at], preferred_element_type=f32)
-                        * adapter_scale).astype(bf16)
-        return 0
-
-    lax.fori_loop(0, cols // tile, up_tile, 0)
-
-    def send_back(d, _):
-        to = lax.rem(me + d, GROUPS)
-        remote(block(delta, to), block(back, me), bs.at[to], br.at[me], to, z).start()
-        return 0
-
-    lax.fori_loop(1, GROUPS, send_back, 0)
-    pltpu.make_async_copy(block(delta, me), block(back, me), br.at[me]).start()
 
     def sum_copy(dy):
         yd = lax.rem(y + dy, NY)
@@ -323,19 +358,26 @@
         return 0
 
     lax.fori_loop(1, nz, sent_z, 0)
-    for part in range(2):
-        for dy in range(NY):
-            for dc in range(NC):
-                if dy or dc:
-                    x_copy(part, dy, dc).wait_send()
-                e_copy(part, dc, dy).wait_send()
+    for dy in range(NY):
+        for dc in range(NC):
+            if dy or dc:
+                x_copy(dy, dc).wait_send()
+            for way in range(2):
+                e_copy(way, dc, dy).wait_send()
+        for way in range(2):
+            h_copy(way, dy).wait_send()
+    for dx in (1, 3):
+        for h in range(2):
+            w_copy(dx, h).wait_send()
     for dx in (1, 2, 3):
-        w_copy(dx).wait_send()
         sum_copy(dx).wait_send()
+    for c in range(NC):
+        w_pass(c).wait_send()
 
     @pl.when(half != core)
     def _():
-        w_copy(0).wait_send()
+        for h in range(2):
+            w_copy(0, h).wait_send()
 
     for dy in range(NY):
         pair_copy(dy).wait_send()
@@ -386,9 +428,10 @@
             dma((GROUPS,)), dma((GROUPS,)),
             dma((nz,)), dma((nz,)),
             dma((nz,)), dma((nz,)),
+            dma((NC, NY)), dma((NC, NY)),
             dma((2, NC, NY)), dma((2, NC, NY)),
-            dma((2, NC, NY)), dma((2, NC, NY)),
-            dma((4,)), dma((4,)),
+            dma((2, NY)), dma((2, NY)),
+            dma((4, 2)), dma((4, 2)), dma((NC,)),
             dma((NY,)), dma((NY,)),
             dma((NY,)), dma((NY,)),
         ],

time: 89.7 us -> 79 us (0.88)
  Pallas kernels: 87.9 us -> 77.2 us
    pallas_call x1, Pallas kernels: 87.9 us -> 77.2 us  [per_device(): pl.pallas_call(functools.partial(kernel, nz), out_shape=jax.ShapeDtypeStr...]
where the time goes in v2:
time: 79 us; the launch traced here: 78.9 us
  Pallas kernels  77.2 us (98%)
  local copies, waits for them, and re-layouts  1.67 us (2%)
    pallas_call x1, Pallas kernels, per_device(): pl.pallas_call(functools.partial(kernel, nz), out_shape=jax.ShapeDtypeStr...  77.2 us
    unnamed x1, local copies, waits for them, and re-layouts  1.67 us

profile of v2, /device:TPU:1, one launch (start us, length us, event | category | flops | bytes accessed | tf_op | source)
XLA Modules:
  0.0 78.9 jit_solution(8607332276837748147)
XLA Ops:
  0.0 77.2 %shard_map.64 = bf16[128,1024]{1,0:T(8,128)(2,1)} custom-call(s32[1,128]{1,0:T(1,128)} %bitcast.5, bf16[128,8192]{1,0:T(8,128)(2,1)} %att.1, bf16[128,1024]{1,0:T(8,128)(2,1)} %res_hbm.1, bf16[256,1024]{1,0:T(8,128)(2,1)} %w_hbm.1, bf16[1024,1024]{1,0:T(8,128)(2,1)} %bitcast.3, bf16[1024,1024]{1,0:T(8,128)(2,1)} %bitcast.4), custom_call_target="tpu_custom_call" | custom-call | tf_op jit(solution)/shard_map/pallas_call | solution.py:400
  77.2 1.7 %copy.8 = bf16[128,1024]{1,0:T(8,128)(2,1)} copy(bf16[128,1024]{1,0:T(8,128)(2,1)} %shard_map.64) | data formatting | bytes 524288

commit v3 on v2

--- a/solution.py
+++ b/solution.py
@@ -40,6 +40,10 @@
     kcols = xb.shape[-1]
     quarter = rows // 4
     wblk = w_hbm.shape[0]
+    hcols = cols // 2
+
+    def part_of(g):
+        return pl.ds(g * hcols, hcols)
 
     def dev(yy, xx, cc):
         return (yy * NX + xx) * NC + cc
@@ -75,6 +79,111 @@
 
     lax.fori_loop(1, nz, greet_z, 0)
 
+    pl.semaphore_wait(barrier, GROUPS - 1 + nz - 1)
+
+    def block(ref, i):
+        return ref.at[pl.ds(pl.multiple_of(i * CAP, CAP), CAP), :]
+
+    def fwd_copy(to):
+        return remote(block(fwd, to), block(got, me), fs.at[to], fr.at[me], to, z)
+
+    def x_copy(dy, dc):
+        yd = lax.rem(y + dy, NY)
+        cd = lax.rem(core + dc, NC)
+        src = att.at[pl.ds(pl.multiple_of(mine_q * quarter, quarter), quarter),
+                     pl.ds(pl.multiple_of((yd * NC + cd) * kcols, kcols), kcols)]
+        dst = xb.at[mine_q, dc, y]
+        if dy == 0 and dc == 0:
+            return pltpu.make_async_copy(src, dst, xr.at[dc, y])
+        return remote(src, dst, xs.at[dc, dy], xr.at[dc, y], dev(yd, x, cd), z)
+
+    def send_x():
+        for dy in (2, 1, 3, 0):
+            for dc in range(NC):
+                x_copy(dy, dc).start()
+
+    send_x()
+    half = lax.div(x, 2)
+    spot = lax.rem(x, 2) * NC + core
+    hblk = wblk // 2
+
+    def w_part(p, h, g):
+        return wg.at[pl.ds(pl.multiple_of(p * wblk + h * hblk, hblk), hblk), part_of(g)]
+
+    def w_copy(dx, h, g):
+        return remote(w_hbm.at[pl.ds(h * hblk, hblk), part_of(g)], w_part(spot, h, g),
+                      ws.at[dx, h, g], wr.at[spot, h, g], dev(y, lax.rem(x + dx, NX), half), z)
+
+    def send_w(g):
+        for i in range(2):
+            w_copy(1, i, g).start()
+            w_copy(3, 1 - i, g).start()
+
+        @pl.when(half == core)
+        def _():
+            for h in range(2):
+                pltpu.make_async_copy(w_hbm.at[pl.ds(h * hblk, hblk), part_of(g)],
+                                      w_part(spot, h, g), wr.at[spot, h, g]).start()
+
+        @pl.when(half != core)
+        def _():
+            for h in range(2):
+                w_copy(0, h, g).start()
+
+    ahead = lax.rem(x - 2 * core + NX, NX)
+    near = lax.rem(ahead + 1, 2)
+    side = 1 - lax.rem(lax.div(ahead + 1, 2), 2)
+
+    def w_pass(c, g):
+        part = w_part(near * NC + c, side, g)
+        return remote(part, part, vs.at[c, g], wr.at[near * NC + c, side, g],
+                      dev(y, lax.rem(x + 1 + 2 * side, NX), core), z)
+
+    def w_arrived(p, h, g):
+        part = w_part(p, h, g)
+        pltpu.make_async_copy(part, part, wr.at[p, h, g]).wait()
+
+    def pass_on(g):
+        for c in range(NC):
+            w_arrived(near * NC + c, side, g)
+            w_pass(c, g).start()
+
+    def w_ready(g):
+        for c in range(NC):
+            w_arrived(near * NC + c, 1 - side, g)
+            w_arrived((1 - near) * NC + c, 0, g)
+            w_arrived((1 - near) * NC + c, 1, g)
+
+    right, left = lax.rem(z + 1, nz), lax.rem(z + nz - 1, nz)
+    left_q, right_q, far_q = lax.rem(mine_q + 3, 4), lax.rem(mine_q + 1, 4), lax.rem(mine_q + 2, 4)
+
+    def e_copy(way, rel, yy):
+        ref = xb.at[mine_q, rel, yy]
+        return remote(ref, ref, es.at[way, rel, yy], er.at[way, rel, yy], me, (right, left)[way])
+
+    def h_copy(way, yy):
+        ref = xb.at[(left_q, right_q)[way], way, yy]
+        return remote(ref, ref, hs.at[way, yy], hr.at[way, yy], me, (right, left)[way])
+
+    def arrived(q, rel, yy, sem):
+        ref = xb.at[q, rel, yy]
+        pltpu.make_async_copy(ref, ref, sem).wait()
+
+    def share(i, _):
+        yy = lax.rem(i, NY)
+        rel = lax.div(i, NY)
+        arrived(mine_q, rel, yy, xr.at[rel, yy])
+        e_copy(0, rel, yy).start()
+        e_copy(1, rel, yy).start()
+        return 0
+
+    def share_on(yy, _):
+        for way in range(2):
+            arrived((left_q, right_q)[way], way, yy, er.at[way, way, yy])
+            h_copy(way, yy).start()
+        return 0
+
+    send_w(0)
     ids = idx_ref[...]
     owner = lax.shift_right_logical(ids, 4)
     local = lax.bitwise_and(ids, CAP - 1)
@@ -94,110 +203,79 @@
         placing, jnp.broadcast_to(local_col, (rows, META)).astype(bf16),
         preferred_element_type=f32).astype(bf16)
 
-    pl.semaphore_wait(barrier, GROUPS - 1 + nz - 1)
-
-    def block(ref, i):
-        return ref.at[pl.ds(pl.multiple_of(i * CAP, CAP), CAP), :]
-
-    def fwd_copy(to):
-        return remote(block(fwd, to), block(got, me), fs.at[to], fr.at[me], to, z)
-
-    def x_copy(dy, dc):
-        yd = lax.rem(y + dy, NY)
-        cd = lax.rem(core + dc, NC)
-        src = att.at[pl.ds(pl.multiple_of(mine_q * quarter, quarter), quarter),
-                     pl.ds(pl.multiple_of((yd * NC + cd) * kcols, kcols), kcols)]
-        dst = xb.at[mine_q, dc, y]
-        if dy == 0 and dc == 0:
-            return pltpu.make_async_copy(src, dst, xr.at[dc, y])
-        return remote(src, dst, xs.at[dc, dy], xr.at[dc, y], dev(yd, x, cd), z)
-
-    def send_x():
-        for dy in (2, 1, 3, 0):
-            for dc in range(NC):
-                x_copy(dy, dc).start()
-
-    send_x()
     for dy, dx, dc in FAR_FIRST:
         fwd_copy(dev(lax.rem(y + dy, NY), lax.rem(x + dx, NX), lax.rem(core + dc, NC))).start()
     pltpu.make_async_copy(block(fwd, me), block(got, me), fr.at[me]).start()
 
-    half = lax.div(x, 2)
-    spot = lax.rem(x, 2) * NC + core
-    hblk = wblk // 2
-
-    def w_part(p, h):
-        return wg.at[pl.ds(pl.multiple_of(p * wblk + h * hblk, hblk), hblk), :]
-
-    def w_copy(dx, h):
-        return remote(w_hbm.at[pl.ds(h * hblk, hblk), :], w_part(spot, h), ws.at[dx, h],
-                      wr.at[spot, h], dev(y, lax.rem(x + dx, NX), half), z)
-
-    def send_w():
-        for i in range(2):
-            w_copy(1, i).start()
-            w_copy(3, 1 - i).start()
-
-        @pl.when(half == core)
-        def _():
-            for h in range(2):
-                pltpu.make_async_copy(w_hbm.at[pl.ds(h * hblk, hblk), :], w_part(spot, h),
-                                      wr.at[spot, h]).start()
-
-        @pl.when(half != core)
-        def _():
-            for h in range(2):
-                w_copy(0, h).start()
-
-    ahead = lax.rem(x - 2 * core + NX, NX)
-    near = lax.rem(ahead + 1, 2)
-    side = 1 - lax.rem(lax.div(ahead + 1, 2), 2)
-
-    def w_pass(c):
-        part = w_part(near * NC + c, side)
-        return remote(part, part, vs.at[c], wr.at[near * NC + c, side],
-                      dev(y, lax.rem(x + 1 + 2 * side, NX), core), z)
-
-    def w_arrived(p, h):
-        pltpu.make_async_copy(w_part(p, h), w_part(p, h), wr.at[p, h]).wait()
-
-    right, left = lax.rem(z + 1, nz), lax.rem(z + nz - 1, nz)
-    left_q, right_q, far_q = lax.rem(mine_q + 3, 4), lax.rem(mine_q + 1, 4), lax.rem(mine_q + 2, 4)
-
-    def e_copy(way, rel, yy):
-        ref = xb.at[mine_q, rel, yy]
-        return remote(ref, ref, es.at[way, rel, yy], er.at[way, rel, yy], me, (right, left)[way])
-
-    def h_copy(way, yy):
-        ref = xb.at[(left_q, right_q)[way], way, yy]
-        return remote(ref, ref, hs.at[way, yy], hr.at[way, yy], me, (right, left)[way])
-
-    def arrived(q, rel, yy, sem):
-        ref = xb.at[q, rel, yy]
-        pltpu.make_async_copy(ref, ref, sem).wait()
-
-    def share(i, _):
-        yy = lax.rem(i, NY)
-        rel = lax.div(i, NY)
-        arrived(mine_q, rel, yy, xr.at[rel, yy])
-        e_copy(0, rel, yy).start()
-        e_copy(1, rel, yy).start()
-        return 0
-
-    def share_on(yy, _):
+    lax.fori_loop(0, NY * NC, share, 0)
+    def base(k, g):
+        place = pl.ds(pl.multiple_of(k * quarter, quarter), quarter)
+        tile = min(256, hcols)
+
+        def one(n, _):
+            at = pl.ds(pl.multiple_of(g * hcols + n * tile, tile), tile)
+            r = jnp.dot(xb[k].reshape(NC * NY * quarter, kcols), wg[:, at],
+                        preferred_element_type=f32)
+            r = r.reshape(NC, NY, quarter, tile)
+            keep[:, place, at] = r[0]
+            sib_out[:, place, at] = r[1].astype(bf16)
+            return 0
+
+        lax.fori_loop(0, hcols // tile, one, 0)
+
+    def from_sides(yy, _):
+        arrived(left_q, 1, yy, er.at[0, 1, yy])
+        arrived(right_q, 0, yy, er.at[1, 0, yy])
+        return 0
+
+    def from_far(yy, _):
         for way in range(2):
-            arrived((left_q, right_q)[way], way, yy, er.at[way, way, yy])
-            h_copy(way, yy).start()
-        return 0
-
-    lax.fori_loop(0, NY * NC, share, 0)
-    send_w()
+            arrived(far_q, way, yy, hr.at[way, yy])
+        return 0
+
+    def pair_copy(yy, g):
+        return remote(sib_out.at[yy, :, part_of(g)], sib_in.at[yy, :, part_of(g)], ps.at[yy, g],
+                      pr.at[yy, g], dev(y, x, 1 - core), z)
+
+    def sum_copy(dy, g):
+        yd = lax.rem(y + dy, NY)
+        return remote(sum_out.at[dy, :, part_of(g)], sum_in.at[dy, :, part_of(g)], rs.at[dy, g],
+                      rr.at[dy, g], dev(yd, x, core), z)
+
+    def project_base(g):
+        w_ready(g)
+        base(mine_q, g)
+        if g == 0:
+            lax.fori_loop(0, NY, from_sides, 0)
+        base(left_q, g)
+        base(right_q, g)
+        if g == 0:
+            lax.fori_loop(0, NY, from_far, 0)
+        base(far_q, g)
+        for dy in (2, 1, 3, 0):
+            pair_copy(lax.rem(y + dy, NY), g).start()
+
+    def send_sum(g):
+        at = slice(g * hcols, (g + 1) * hcols)
+        for dy in (2, 1, 3, 0):
+            yd = lax.rem(y + dy, NY)
+            ref = sib_in.at[yd, :, part_of(g)]
+            pltpu.make_async_copy(ref, ref, pr.at[yd, g]).wait()
+            if dy == 0:
+                keep[yd, :, at] = keep[yd, :, at] + sib_in[yd, :, at].astype(f32)
+            else:
+                sum_out[dy, :, at] = (keep[yd, :, at] + sib_in[yd, :, at].astype(f32)).astype(bf16)
+                sum_copy(dy, g).start()
+
+    pass_on(0)
+    lax.fori_loop(0, NY, share_on, 0)
 
     def got_fwd(s, _):
         pltpu.make_async_copy(block(got, s), block(got, s), fr.at[s]).wait()
         return 0
 
     lax.fori_loop(0, GROUPS, got_fwd, 0)
+    send_w(1)
     load_down.wait()
     lane = iota((slots, 128), 1)
     mine = got[:, cols:].astype(f32) - (lane >= 64).astype(f32)
@@ -219,25 +297,6 @@
 
     lax.fori_loop(1, nz, low_send, 0)
 
-    def base(k):
-        place = pl.ds(pl.multiple_of(k * quarter, quarter), quarter)
-        tile = min(256, cols)
-
-        def one(n, _):
-            at = pl.ds(pl.multiple_of(n * tile, tile), tile)
-            r = jnp.dot(xb[k].reshape(NC * NY * quarter, kcols), wg[:, at],
-                        preferred_element_type=f32)
-            r = r.reshape(NC, NY, quarter, tile)
-            keep[:, place, at] = r[0]
-            sib_out[:, place, at] = r[1].astype(bf16)
-            return 0
-
-        lax.fori_loop(0, cols // tile, one, 0)
-
-    for c in range(NC):
-        w_arrived(near * NC + c, side)
-        w_pass(c).start()
-
     def low_got(d, total):
         s = lax.rem(z + d, nz)
         pltpu.make_async_copy(low_in.at[s], low_in.at[s], lr.at[s]).wait()
@@ -282,55 +341,18 @@
             remote(block(delta, to), block(back, me), bs.at[to], br.at[me], to, z).start()
         pltpu.make_async_copy(block(delta, me), block(back, me), br.at[me]).start()
 
+    project_base(0)
+    pass_on(1)
+    send_sum(0)
     up_and_back()
-    lax.fori_loop(0, NY, share_on, 0)
-
-    for c in range(NC):
-        w_arrived(near * NC + c, 1 - side)
-        w_arrived((1 - near) * NC + c, 0)
-        w_arrived((1 - near) * NC + c, 1)
-    base(mine_q)
-
-    def from_sides(yy, _):
-        arrived(left_q, 1, yy, er.at[0, 1, yy])
-        arrived(right_q, 0, yy, er.at[1, 0, yy])
-        return 0
-
-    lax.fori_loop(0, NY, from_sides, 0)
-    base(left_q)
-    base(right_q)
-
-    def from_far(yy, _):
-        for way in range(2):
-            arrived(far_q, way, yy, hr.at[way, yy])
-        return 0
-
-    lax.fori_loop(0, NY, from_far, 0)
-    base(far_q)
-
-    def pair_copy(yy):
-        return remote(sib_out.at[yy], sib_in.at[yy], ps.at[yy], pr.at[yy],
-                      dev(y, x, 1 - core), z)
-
-    for dy in (2, 1, 3, 0):
-        pair_copy(lax.rem(y + dy, NY)).start()
-
-    def sum_copy(dy):
-        yd = lax.rem(y + dy, NY)
-        return remote(sum_out.at[dy], sum_in.at[dy], rs.at[dy], rr.at[dy], dev(yd, x, core), z)
-
-    for dy in (2, 1, 3, 0):
-        yd = lax.rem(y + dy, NY)
-        pltpu.make_async_copy(sib_in.at[yd], sib_in.at[yd], pr.at[yd]).wait()
-        if dy == 0:
-            keep[yd] = keep[yd] + sib_in[yd].astype(f32)
-        else:
-            sum_out[dy] = (keep[yd] + sib_in[yd].astype(f32)).astype(bf16)
-            sum_copy(dy).start()
+    project_base(1)
+    send_sum(1)
 
     load_res.wait()
-    for dy in (1, 3, 2):
-        pltpu.make_async_copy(sum_in.at[dy], sum_in.at[dy], rr.at[dy]).wait()
+    for g in range(2):
+        for dy in (1, 3, 2):
+            ref = sum_in.at[dy, :, part_of(g)]
+            pltpu.make_async_copy(ref, ref, rr.at[dy, g]).wait()
     total = (res[...].astype(f32) + keep[y] + sum_in[1].astype(f32) + sum_in[2].astype(f32)
              + sum_in[3].astype(f32))
     homing = (iota((rows, slots), 1) == target_col.astype(i32)).astype(bf16)
@@ -366,21 +388,22 @@
                 e_copy(way, dc, dy).wait_send()
         for way in range(2):
             h_copy(way, dy).wait_send()
-    for dx in (1, 3):
-        for h in range(2):
-            w_copy(dx, h).wait_send()
-    for dx in (1, 2, 3):
-        sum_copy(dx).wait_send()
-    for c in range(NC):
-        w_pass(c).wait_send()
+    for g in range(2):
+        for dx in (1, 3):
+            for h in range(2):
+                w_copy(dx, h, g).wait_send()
+        for dx in (1, 2, 3):
+            sum_copy(dx, g).wait_send()
+        for c in range(NC):
+            w_pass(c, g).wait_send()
+        for dy in range(NY):
+            pair_copy(dy, g).wait_send()
 
     @pl.when(half != core)
     def _():
-        for h in range(2):
-            w_copy(0, h).wait_send()
-
-    for dy in range(NY):
-        pair_copy(dy).wait_send()
+        for g in range(2):
+            for h in range(2):
+                w_copy(0, h, g).wait_send()
 
 
 def per_device(
@@ -431,9 +454,9 @@
             dma((NC, NY)), dma((NC, NY)),
             dma((2, NC, NY)), dma((2, NC, NY)),
             dma((2, NY)), dma((2, NY)),
-            dma((4, 2)), dma((4, 2)), dma((NC,)),
-            dma((NY,)), dma((NY,)),
-            dma((NY,)), dma((NY,)),
+            dma((4, 2, 2)), dma((4, 2, 2)), dma((NC, 2)),
+            dma((NY, 2)), dma((NY, 2)),
+            dma((NY, 2)), dma((NY, 2)),
         ],
         compiler_params=pltpu.CompilerParams(
             collective_id=0, has_side_effects=True, vmem_limit_bytes=60 * 1024 * 1024),

time: 79 us -> 75.5 us (0.956)
  Pallas kernels: 77.2 us -> 73.2 us
    pallas_call x1, Pallas kernels: 77.2 us -> 73.2 us  [per_device(): pl.pallas_call(functools.partial(kernel, nz), out_shape=jax.ShapeDtypeStr...]
where the time goes in v3:
time: 75.5 us; the launch traced here: 74.9 us
  Pallas kernels  73.2 us (97%)
  local copies, waits for them, and re-layouts  1.67 us (2%)
    pallas_call x1, Pallas kernels, per_device(): pl.pallas_call(functools.partial(kernel, nz), out_shape=jax.ShapeDtypeStr...  73.2 us
    unnamed x1, local copies, waits for them, and re-layouts  1.67 us

profile of v3, /device:TPU:1, one launch (start us, length us, event | category | flops | bytes accessed | tf_op | source)
XLA Modules:
  0.0 74.9 jit_solution(14040740420971407560)
XLA Ops:
  0.0 73.2 %shard_map.64 = bf16[128,1024]{1,0:T(8,128)(2,1)} custom-call(s32[1,128]{1,0:T(1,128)} %bitcast.5, bf16[128,8192]{1,0:T(8,128)(2,1)} %att.1, bf16[128,1024]{1,0:T(8,128)(2,1)} %res_hbm.1, bf16[256,1024]{1,0:T(8,128)(2,1)} %w_hbm.1, bf16[1024,1024]{1,0:T(8,128)(2,1)} %bitcast.3, bf16[1024,1024]{1,0:T(8,128)(2,1)} %bitcast.4), custom_call_target="tpu_custom_call" | custom-call | tf_op jit(solution)/shard_map/pallas_call | solution.py:423
  73.2 1.7 %copy.8 = bf16[128,1024]{1,0:T(8,128)(2,1)} copy(bf16[128,1024]{1,0:T(8,128)(2,1)} %shard_map.64) | data formatting | bytes 524288

commit v4 on v3

--- a/solution.py
+++ b/solution.py
@@ -15,7 +15,7 @@
 MESH = pl.DeviceIdType.MESH
 FAR_FIRST = sorted(
     ((dy, dx, dc) for dy in range(NY) for dx in range(NX) for dc in range(NC) if dy or dx or dc),
-    key=lambda o: -min(o[0], NY - o[0]) - min(o[1], NX - o[1]))
+    key=lambda o: (-min(o[0], NY - o[0]) - min(o[1], NX - o[1]), o[2]))
 f32, bf16, i32 = jnp.float32, jnp.bfloat16, jnp.int32
 
 
@@ -203,6 +203,7 @@
         placing, jnp.broadcast_to(local_col, (rows, META)).astype(bf16),
         preferred_element_type=f32).astype(bf16)
 
+    pass_on(0)
     for dy, dx, dc in FAR_FIRST:
         fwd_copy(dev(lax.rem(y + dy, NY), lax.rem(x + dx, NX), lax.rem(core + dc, NC))).start()
     pltpu.make_async_copy(block(fwd, me), block(got, me), fr.at[me]).start()
@@ -249,6 +250,8 @@
             lax.fori_loop(0, NY, from_sides, 0)
         base(left_q, g)
         base(right_q, g)
+
+    def project_far(g):
         if g == 0:
             lax.fori_loop(0, NY, from_far, 0)
         base(far_q, g)
@@ -267,8 +270,8 @@
                 sum_out[dy, :, at] = (keep[yd, :, at] + sib_in[yd, :, at].astype(f32)).astype(bf16)
                 sum_copy(dy, g).start()
 
-    pass_on(0)
     lax.fori_loop(0, NY, share_on, 0)
+    project_base(0)
 
     def got_fwd(s, _):
         pltpu.make_async_copy(block(got, s), block(got, s), fr.at[s]).wait()
@@ -296,6 +299,7 @@
         return 0
 
     lax.fori_loop(1, nz, low_send, 0)
+    project_far(0)
 
     def low_got(d, total):
         s = lax.rem(z + d, nz)
@@ -341,11 +345,11 @@
             remote(block(delta, to), block(back, me), bs.at[to], br.at[me], to, z).start()
         pltpu.make_async_copy(block(delta, me), block(back, me), br.at[me]).start()
 
-    project_base(0)
     pass_on(1)
     send_sum(0)
     up_and_back()
     project_base(1)
+    project_far(1)
     send_sum(1)
 
     load_res.wait()

time: 75.5 us -> 72.9 us (0.966)
  Pallas kernels: 73.2 us -> 71.1 us
    pallas_call x1, Pallas kernels: 73.2 us -> 71.1 us  [per_device(): pl.pallas_call(functools.partial(kernel, nz), out_shape=jax.ShapeDtypeStr...]
where the time goes in v4:
time: 72.9 us; the launch traced here: 72.7 us
  Pallas kernels  71.1 us (98%)
  local copies, waits for them, and re-layouts  1.67 us (2%)
    pallas_call x1, Pallas kernels, per_device(): pl.pallas_call(functools.partial(kernel, nz), out_shape=jax.ShapeDtypeStr...  71.1 us
    unnamed x1, local copies, waits for them, and re-layouts  1.67 us

profile of v4, /device:TPU:1, one launch (start us, length us, event | category | flops | bytes accessed | tf_op | source)
XLA Modules:
  0.0 72.7 jit_solution(5135495287842227815)
XLA Ops:
  0.0 71.1 %shard_map.64 = bf16[128,1024]{1,0:T(8,128)(2,1)} custom-call(s32[1,128]{1,0:T(1,128)} %bitcast.5, bf16[128,8192]{1,0:T(8,128)(2,1)} %att.1, bf16[128,1024]{1,0:T(8,128)(2,1)} %res_hbm.1, bf16[256,1024]{1,0:T(8,128)(2,1)} %w_hbm.1, bf16[1024,1024]{1,0:T(8,128)(2,1)} %bitcast.3, bf16[1024,1024]{1,0:T(8,128)(2,1)} %bitcast.4), custom_call_target="tpu_custom_call" | custom-call | tf_op jit(solution)/shard_map/pallas_call | solution.py:427
  71.1 1.7 %copy.8 = bf16[128,1024]{1,0:T(8,128)(2,1)} copy(bf16[128,1024]{1,0:T(8,128)(2,1)} %shard_map.64) | data formatting | bytes 524288
